TPU v7x, 32 devices: a whole 2x2x4 slice. The times are simulated.
32 devices in a mesh: grp: 4 (over y, x), row: 8 (over z, core).
Axes of the slice: x: 2, y: 2, z: 4, core: 2. Of those that a mesh axis runs over, the one named last changes fastest.
Arguments:
- snapshots: float32 [16, 4, 65536], P('grp', None, 'row'), may hold values from -12 to 12
- basis: float32 [128, 262144], P(None, ('grp', 'row')), may hold values from -4 to 4
- assignment: int32 [16], replicated, may hold values from 0 to 15, each once
- param_index: int32 [16], replicated, may hold values from 0 to 63
- offsets: int32 [8, 262144], P(None, ('grp', 'row')), may hold values from -2048 to 2048, as said below
- coefs: float32 [2, 8, 262144], P(None, None, ('grp', 'row')), may hold values from -2.5 to 2.5
Outputs:
- new_columns: float32 [16, 262144], P(None, ('grp', 'row'))
- applied: float32 [2, 16, 262144], P(None, None, ('grp', 'row'))
- coords: float32 [128, 16], replicated
- r_factor: float32 [16, 16], replicated
- reduced: float32 [2, 144, 16], replicated
- estimate: float32 [16], replicated
Inputs may be any that keep to these rules, and one draw needn't show every extreme that they name: `offsets`: both ends of the range occur in every draw.
All inputs are finite; a program needn't handle non-finite values.
Results may differ from a plain program's by a relative error of at most 0.00029.
Values sent between devices are 32-bit elements; how exact they have to be, the bound alone decides.
A program may use at most 64 MiB of HBM per device.

v0:
```python
import jax
import jax.numpy as jnp
from jax import lax
from jax.sharding import PartitionSpec as P

NPARAM = 64


def extended_2(block, sides, width):
    for axis, dim in sides:
        count = lax.axis_size(axis)
        forward = [(i, i + 1) for i in range(count - 1)]
        backward = [(target, source) for source, target in forward]
        low = lax.ppermute(
            lax.slice_in_dim(block, block.shape[dim] - width, None, axis=dim), axis, forward
        )
        high = lax.ppermute(lax.slice_in_dim(block, 0, width, axis=dim), axis, backward)
        block = jnp.concatenate([low, block, high], axis=dim)
    return block


def cholesky_lower(matrix):
    order = matrix.shape[0]
    index_list = jnp.arange(order, dtype=jnp.int32)

    def cholesky_step(column_index, factor):
        column = lax.dynamic_slice_in_dim(matrix, column_index, 1, 1)[:, 0]
        factor_row = lax.dynamic_slice_in_dim(factor, column_index, 1, 0)[0]
        column = column - jnp.dot(factor, factor_row, precision=lax.Precision.HIGHEST)
        pivot = jnp.sqrt(jnp.sum(jnp.where(index_list == column_index, column, 0.0)))
        fresh = jnp.where(
            index_list > column_index,
            column / pivot,
            jnp.where(index_list == column_index, pivot, 0.0),
        )
        return lax.dynamic_update_slice_in_dim(factor, fresh[:, None], column_index, 1)

    return lax.fori_loop(0, order, cholesky_step, jnp.zeros(matrix.shape, matrix.dtype))


def forward_solve(lower, right):
    order = lower.shape[0]

    def forward_step(row_index, solved):
        lower_row = lax.dynamic_slice_in_dim(lower, row_index, 1, 0)[0]
        pivot = jnp.sum(jnp.where(jnp.arange(order, dtype=jnp.int32) == row_index, lower_row, 0.0))
        target = lax.dynamic_slice_in_dim(right, row_index, 1, 0)[0]
        value = (target - jnp.dot(lower_row, solved, precision=lax.Precision.HIGHEST)) / pivot
        return lax.dynamic_update_slice_in_dim(solved, value[None, :], row_index, 0)

    return lax.fori_loop(0, order, forward_step, jnp.zeros(right.shape, right.dtype))


def backward_solve(lower, right):
    order = lower.shape[0]

    def backward_step(turn, solved):
        row_index = order - 1 - turn
        upper_row = lax.dynamic_slice_in_dim(lower, row_index, 1, 1)[:, 0]
        pivot = jnp.sum(jnp.where(jnp.arange(order, dtype=jnp.int32) == row_index, upper_row, 0.0))
        target = lax.dynamic_slice_in_dim(right, row_index, 1, 0)[0]
        value = (target - jnp.dot(upper_row, solved, precision=lax.Precision.HIGHEST)) / pivot
        return lax.dynamic_update_slice_in_dim(solved, value[None, :], row_index, 0)

    return lax.fori_loop(0, order, backward_step, jnp.zeros(right.shape, right.dtype))


def apply_local(extended, offsets, coefs, width):
    row_count = offsets.shape[1]
    positions = jnp.arange(row_count, dtype=jnp.int32) + width
    totals = [
        jnp.zeros((extended.shape[0], row_count), jnp.float32)
        for term_index in range(coefs.shape[0])
    ]
    for slot_index in range(offsets.shape[0]):
        picked = jnp.take(extended, positions + offsets[slot_index], axis=1)
        totals = [
            totals[term_index] + coefs[term_index, slot_index][None, :] * picked
            for term_index in range(len(totals))
        ]
    return jnp.stack(totals)


def body(snapshots, basis, assignment, param_index, offsets, coefs):
    highest = lax.Precision.HIGHEST
    snap_count = assignment.shape[0]
    local_rows = basis.shape[1]
    total_rows = local_rows * lax.axis_size("grp") * lax.axis_size("row")
    width = local_rows // 4
    received = lax.all_to_all(snapshots, "grp", split_axis=1, concat_axis=0, tiled=True)
    arrived = received.reshape(snap_count, local_rows)
    placing = (assignment[None, :] == jnp.arange(snap_count, dtype=jnp.int32)[:, None]).astype(
        jnp.float32
    )
    ordered = jnp.dot(placing, arrived, precision=highest)
    gram = lax.psum(jnp.dot(basis, basis.T, precision=highest), ("grp", "row")) / total_rows
    basis_lower = cholesky_lower(gram)
    project_sum, snap_sum = lax.psum(
        (
            jnp.dot(basis, ordered.T, precision=highest),
            jnp.dot(ordered, ordered.T, precision=highest),
        ),
        ("grp", "row"),
    )
    project = project_sum / total_rows
    halfway = forward_solve(basis_lower, project)
    coords = backward_solve(basis_lower, halfway)
    residual = ordered - jnp.dot(coords.T, basis, precision=highest)
    cross = jnp.dot(project.T, coords, precision=highest)
    curved = jnp.dot(coords.T, jnp.dot(gram, coords, precision=highest), precision=highest)
    residual_gram = snap_sum / total_rows - cross - cross.T + curved
    residual_gram = 0.5 * (residual_gram + residual_gram.T)
    lower = cholesky_lower(residual_gram)
    inverse = forward_solve(lower, jnp.eye(snap_count, dtype=jnp.float32))
    new_columns = jnp.dot(inverse, residual, precision=highest)
    extended = extended_2(new_columns, ((("grp", "row"), 1),), width)
    applied = apply_local(extended, offsets, coefs, width)
    blocks = []
    for term_index in range(coefs.shape[0]):
        upper_part = jnp.dot(basis, applied[term_index].T, precision=highest)
        lower_part = jnp.dot(new_columns, applied[term_index].T, precision=highest)
        blocks.append(jnp.concatenate([upper_part, lower_part], axis=0))
    viscosity = 0.5 + param_index.astype(jnp.float32) / NPARAM
    combined = applied[0]
    term_index = 1
    combined = combined + (viscosity**term_index)[:, None] * applied[term_index]
    block_sum, square_sum = lax.psum(
        (jnp.stack(blocks), jnp.sum(combined * combined, axis=1)), ("grp", "row")
    )
    reduced = block_sum / total_rows
    estimate = square_sum / total_rows
    return (new_columns, applied, coords, lower.T, reduced, estimate)


def solution(mesh):
    return jax.shard_map(
        body,
        mesh=mesh,
        in_specs=(
            P("grp", None, "row"),
            P(None, ("grp", "row")),
            P(),
            P(),
            P(None, ("grp", "row")),
            P(None, None, ("grp", "row")),
        ),
        out_specs=(P(None, ("grp", "row")), P(None, None, ("grp", "row")), P(), P(), P(), P()),
        check_vma=False,
    )
```

profile of v0, /device:TPU:0, one launch (start us, length us, event | category | flops | bytes accessed | tf_op | source)
XLA Modules:
  0.0 1223.7 jit_solution(2992273450105122434)
XLA Ops:
  7.2 2.2 copy.74
  9.3 5.2 all-to-all-start
  14.6 7.6 fusion.64
  24.5 1.1 fusion.60
  25.6 116.0 %all-reduce.4.cloned.1.call-done = f32[128,128]{1,0:T(8,128)} async-done(((f32[128,128]{1,0:T(8,128)}), f32[128,128]{1,0:T(8,128)}) %all-reduce.4.cloned.1.call-update) | async-done | bytes 65552 | tf_op jit(solution)/shard_map/psum | solution.py:96
  141.6 0.8 broadcast_multiply_fusion
  142.6 258.7 %while.74 = (s32[]{:T(128)}, f32[128,128]{1,0:T(8,128)S(1)}, f32[128,128]{0,1:T(8,128)S(1)}, s32[]{:T(128)}, s32[]{:T(128)}) while((s32[]{:T(128)}, f32[128,128]{1,0:T(8,128)S(1)}, f32[128,128]{0,1:T(8,128)S(1)}, s32[]{:T(128)}, s32[]{:T(128)}) %tuple.200), condition=%wide.region_5.6_spmd.clone.clone, body=%wide.region_3.5_spmd.clone.clone.sunk | while | flops 197761 | bytes 71765 | solution.py:38
  142.6 0.8 fusion.125
  144.5 0.8 fusion.125
  146.6 0.8 fusion.125
  148.6 0.8 fusion.125
  150.6 0.8 fusion.125
  152.6 0.8 fusion.125
  154.6 0.8 fusion.125
  156.7 0.8 fusion.125
  158.7 0.8 fusion.125
  160.7 0.8 fusion.125
  162.7 0.8 fusion.125
  164.8 0.8 fusion.125
  166.8 0.8 fusion.125
  168.8 0.8 fusion.125
  170.8 0.8 fusion.125
  172.8 0.8 fusion.125
  174.9 0.8 fusion.125
  176.9 0.8 fusion.125
  178.9 0.8 fusion.125
  180.9 0.8 fusion.125
  183.0 0.8 fusion.125
  185.0 0.8 fusion.125
  187.0 0.8 fusion.125
  189.0 0.8 fusion.125
  191.0 0.8 fusion.125
  193.1 0.8 fusion.125
  402.0 5.1 convolution_bitcast_fusion.7
  407.9 41.0 %all-reduce.1 = (f32[128,16]{0,1:T(8,128)S(1)}, f32[16,16]{1,0:T(8,128)S(1)}) all-reduce(f32[128,16]{0,1:T(8,128)S(1)} %convolution_bitcast_fusion.7, f32[16,16]{1,0:T(8,128)S(1)} %fusion.63), channel_id=1, replica_groups=mesh['grp'=4,'row'=8] {'grp','row'}, use_global_device_ids=true, to_apply=%region_1.2 | all-reduce | flops 2304 | bytes 18432 | tf_op jit(solution)/shard_map/psum | solution.py:98
  449.0 186.3 %while.71 = (s32[]{:T(128)}, f32[128,16]{1,0:T(8,128)S(1)}, f32[128,16]{1,0:T(8,128)S(1)}, f32[128,128]{1,0:T(8,128)S(1)}, s32[]{:T(128)}, /*index=5*/s32[]{:T(128)}) while((s32[]{:T(128)}, f32[128,16]{1,0:T(8,128)S(1)}, f32[128,16]{1,0:T(8,128)S(1)}, f32[128,128]{1,0:T(8,128)S(1)}, s32[]{:T(128)}, /*index=5*/s32[]{:T(128)}) %tuple.203), condition=%wide.region_8.9_spmd, body=%wide.region_6.8_spmd.sunk | while | flops 24993 | bytes 69901 | solution.py:51
  635.3 187.1 %while.72 = (s32[]{:T(128)}, f32[128,16]{1,0:T(8,128)S(1)}, f32[128,16]{1,0:T(8,128)S(1)}, f32[128,128]{0,1:T(8,128)S(1)}, s32[]{:T(128)}, /*index=5*/s32[]{:T(128)}, s32[]{:T(128)}, s32[]{:T(128)}) while((s32[]{:T(128)}, f32[128,16]{1,0:T(8,128)S(1)}, f32[128,16]{1,0:T(8,128)S(1)}, f32[128,128]{0,1:T(8,128)S(1)}, s32[]{:T(128)}, ...), condition=%wide.region_11.12_spmd, body=%wide.region_9.11_spmd.sunk | while | flops 24997 | bytes 68439 | solution.py:65
  822.6 3.8 convolution_subtract_fusion
  827.2 26.0 %while.75 = (s32[]{:T(128)}, f32[16,16]{1,0:T(8,128)S(1)}, f32[16,16]{0,1:T(8,128)S(1)}, s32[]{:T(128)}, s32[]{:T(128)}) while((s32[]{:T(128)}, f32[16,16]{1,0:T(8,128)S(1)}, f32[16,16]{0,1:T(8,128)S(1)}, s32[]{:T(128)}, s32[]{:T(128)}) %tuple.209), condition=%wide.region_14.15_spmd.clone.clone, body=%wide.region_12.14_spmd.clone.clone.sunk | while | flops 3217 | bytes 11285 | solution.py:38
  853.2 22.8 %while.73 = (s32[]{:T(128)}, f32[16,16]{1,0:T(8,128)S(1)}, f32[16,16]{1,0:T(8,128)S(1)}, f32[16,16]{1,0:T(8,128)S(1)}, s32[]{:T(128)}, /*index=5*/s32[]{:T(128)}) while((s32[]{:T(128)}, f32[16,16]{1,0:T(8,128)S(1)}, f32[16,16]{1,0:T(8,128)S(1)}, f32[16,16]{1,0:T(8,128)S(1)}, s32[]{:T(128)}, /*index=5*/s32[]{:T(128)}) %tuple.212), condition=%wide.region_17.18_spmd, body=%wide.region_15.17_spmd.sunk | while | flops 3153 | bytes 12109 | solution.py:51
  876.6 1.3 collective-permute-start
  877.9 1.5 collective-permute-start.1
  881.4 4.0 copy.81
  885.3 30.5 %gather_fusion = f32[8192,16]{1,0:T(8,128)} fusion(f32[16,12288]{0,1:T(8,128)} %copy.81, s32[8192]{0:T(1024)S(1)} %fusion.44), kind=kCustom, calls=%fused_computation.clone | custom fusion | bytes 1081344 | tf_op jit(solution)/shard_map/jit(_take)/gather | solution.py:76
  915.8 2.8 copy.82
  918.6 30.5 %gather_fusion.1 = f32[8192,16]{1,0:T(8,128)} fusion(f32[16,12288]{0,1:T(8,128)} %copy.81, s32[8192]{0:T(1024)S(1)} %fusion.45), kind=kCustom, calls=%fused_computation.1.clone | custom fusion | bytes 1081344 | tf_op jit(solution)/shard_map/jit(_take)/gather | solution.py:76
  949.1 2.8 copy.84
  951.9 30.5 %gather_fusion.2 = f32[8192,16]{1,0:T(8,128)} fusion(f32[16,12288]{0,1:T(8,128)} %copy.81, s32[8192]{0:T(1024)S(1)} %fusion.46), kind=kCustom, calls=%fused_computation.2.clone | custom fusion | bytes 1081344 | tf_op jit(solution)/shard_map/jit(_take)/gather | solution.py:76
  982.3 2.8 copy.86
  985.1 30.5 %gather_fusion.3 = f32[8192,16]{1,0:T(8,128)} fusion(f32[16,12288]{0,1:T(8,128)} %copy.81, s32[8192]{0:T(1024)S(1)} %fusion.47), kind=kCustom, calls=%fused_computation.3.clone | custom fusion | bytes 1081344 | tf_op jit(solution)/shard_map/jit(_take)/gather | solution.py:76
  1015.6 3.5 copy.88
  1019.1 30.5 %gather_fusion.4 = f32[8192,16]{1,0:T(8,128)} fusion(f32[16,12288]{0,1:T(8,128)} %copy.81, s32[8192]{0:T(1024)S(1)} %fusion.48), kind=kCustom, calls=%fused_computation.4.clone | custom fusion | bytes 1081344 | tf_op jit(solution)/shard_map/jit(_take)/gather | solution.py:76
  1049.6 3.5 copy.90
  1053.1 30.5 %gather_fusion.5 = f32[8192,16]{1,0:T(8,128)} fusion(f32[16,12288]{0,1:T(8,128)} %copy.81, s32[8192]{0:T(1024)S(1)} %fusion.49), kind=kCustom, calls=%fused_computation.5.clone | custom fusion | bytes 1081344 | tf_op jit(solution)/shard_map/jit(_take)/gather | solution.py:76
  1083.5 3.5 copy.92
  1087.0 30.5 %gather_fusion.6 = f32[8192,16]{1,0:T(8,128)} fusion(f32[16,12288]{0,1:T(8,128)} %copy.81, s32[8192]{0:T(1024)S(1)} %fusion.50), kind=kCustom, calls=%fused_computation.6.clone | custom fusion | bytes 1081344 | tf_op jit(solution)/shard_map/jit(_take)/gather | solution.py:76
  1117.5 3.5 copy.94
  1121.0 30.5 %gather_fusion.7 = f32[8192,16]{1,0:T(8,128)} fusion(f32[16,12288]{0,1:T(8,128)} %copy.81, s32[8192]{0:T(1024)S(1)} %fusion.51), kind=kCustom, calls=%fused_computation.7.clone | custom fusion | bytes 1081344 | tf_op jit(solution)/shard_map/jit(_take)/gather | solution.py:76
  1151.5 3.5 copy.96
  1155.0 3.5 multiply_reduce_fusion
  1159.3 3.3 convolution_bitcast_fusion.6
  1163.4 3.4 convolution_bitcast_fusion.5
  1166.9 47.8 %all-reduce = (f32[2,144,16]{1,2,0:T(8,128)S(1)}, f32[16]{0:T(128)S(1)}) all-reduce(f32[2,144,16]{1,2,0:T(8,128)S(1)} %pad_maximum_fusion.2, f32[16]{0:T(128)S(1)} %copy-done.7), channel_id=1, replica_groups=mesh['grp'=4,'row'=8] {'grp','row'}, use_global_device_ids=true, to_apply=%region_18.20 | all-reduce | flops 4624 | bytes 36992 | tf_op jit(solution)/shard_map/psum | solution.py:127
  1215.8 1.0 pad_maximum_fusion
  (1437 shorter events, 559.7 us)
Async XLA Ops:
  9.3 392.1 %all-to-all-start = ((f32[4,4,8192]{2,0,1:T(4,128)}), f32[4,4,8192]{2,0,1:T(4,128)S(1)}, u32[]{:S(2)}, u32[]{:S(2)}) async-start(f32[4,4,8192]{2,0,1:T(4,128)} %copy.74), calls=%async_computation | async-start | bytes 1048576 | tf_op jit(solution)/shard_map/all_to_all | solution.py:90
  14.5 7.7 copy-start.3
  14.5 10.0 copy-start.2
  14.5 127.1 %all-reduce.4.cloned.1.call-start = ((), (), s32[]{:S(2)}) async-start(), calls=%async_computation.1 | async-start | bytes 131072 | tf_op jit(solution)/shard_map/psum | solution.py:96
  22.2 379.4 %copy-start.8 = (s32[16]{0:T(128)S(1)}, s32[16]{0:T(128)}, u32[]{:S(2)}) copy-start(s32[16]{0:T(128)} %param.20) | copy-start | bytes 196
  407.1 419.5 %copy-start.4 = (f32[128,128]{1,0:T(8,128)S(1)}, f32[128,128]{1,0:T(8,128)}, u32[]{:S(2)}) copy-start(f32[128,128]{1,0:T(8,128)} %all-reduce.4.cloned.1.call-done) | copy-start | bytes 196612
  635.3 244.1 %copy-start.9 = (s32[16]{0:T(128)S(1)}, s32[16]{0:T(128)}, u32[]{:S(2)}) copy-start(s32[16]{0:T(128)} %param.21) | copy-start | bytes 196
  876.6 286.1 %copy-start.1 = (f32[16,8192]{1,0:T(8,128)}, f32[16,8192]{1,0:T(8,128)S(1)}, u32[]{:S(2)}) copy-start(f32[16,8192]{1,0:T(8,128)S(1)} %fusion.65) | copy-start | bytes 1572868
  876.6 4.7 collective-permute-start
  877.9 3.4 collective-permute-start.1
  1121.0 34.0 %copy-start.5 = (f32[1,1,8192]{2,1,0:T(1,128)S(1)}, f32[1,1,8192]{2,1,0:T(1,128)}, u32[]{:S(2)}) copy-start(f32[1,1,8192]{2,1,0:T(1,128)} %get-tuple-element.621) | copy-start | bytes 98308
  1121.0 34.0 %copy-start.6 = (f32[1,1,8192]{2,1,0:T(1,128)S(1)}, f32[1,1,8192]{2,1,0:T(1,128)}, u32[]{:S(2)}) copy-start(f32[1,1,8192]{2,1,0:T(1,128)} %get-tuple-element.622) | copy-start | bytes 98308
  1155.0 4.3 copy-start
  1159.3 7.6 copy-start.7
Sparse Core Ops, SparseCore 0:
  22.3 119.2 all-reduce.3
where the time goes:
time: 1230 us; the launch traced here: 1220 us
  matrix products  361 us (29%)
  local copies, waits for them, and re-layouts  350 us (28%)
  other arithmetic  175 us (14%)
  waiting for transfers between devices  116 us (9%)
  loops' own time  110 us (9%)
  blocking collectives  88.8 us (7%)
  between operations  14.4 us (1%)
    gather x16, local copies, waits for them, and re-layouts, apply_local(): picked = jnp.take(extended, positions + offsets[slot_index], axis=1)  270 us
    dot_general x144, matrix products, cholesky_step(): jnp.dot(factor, factor_row, precision=lax.Precision.HIGHEST)  117 us
    psum x1, waiting for transfers between devices, body(): lax.psum(jnp.dot(basis, basis.T, precision=highest), ('grp', 'row'))  116 us
    dot_general x144, matrix products, forward_step(): jnp.dot(lower_row, solved, precision=lax.Precision.HIGHEST)  115 us
    another operation x2, loops' own time, cholesky_lower(): lax.fori_loop(0, order, cholesky_step, jnp.zeros(matrix.shape, matrix.dty...  104 us
    dot_general x128, matrix products, backward_step(): jnp.dot(upper_row, solved, precision=lax.Precision.HIGHEST)  102 us
    reduce_sum x144, other arithmetic, forward_step(): jnp.sum(jnp.where(jnp.arange(order, dtype=jnp.int32) == row_index, lower_...  87.3 us
    reduce_sum x128, other arithmetic, backward_step(): jnp.sum(jnp.where(jnp.arange(order, dtype=jnp.int32) == row_index, upper_...  77.7 us
  transfers between devices with their start and end apart: 4, of which 2 were waited for; matrix products, arithmetic and copies ran while one was open for 15% of the time, Pallas kernels for 0%

commit v1 on v0

--- a/solution.py
+++ b/solution.py
@@ -4,6 +4,11 @@
 from jax.sharding import PartitionSpec as P
 
 NPARAM = 64
+
+
+def add_all(value, axis):
+    terms = lax.all_gather(value, axis)
+    return jnp.sum(terms, axis=0)
 
 
 def extended_2(block, sides, width):
@@ -93,7 +98,7 @@
         jnp.float32
     )
     ordered = jnp.dot(placing, arrived, precision=highest)
-    gram = lax.psum(jnp.dot(basis, basis.T, precision=highest), ("grp", "row")) / total_rows
+    gram = add_all(jnp.dot(basis, basis.T, precision=highest), ("grp", "row")) / total_rows
     basis_lower = cholesky_lower(gram)
     project_sum, snap_sum = lax.psum(
         (

time: 1230 us -> 1120 us (0.911)
  waiting for transfers between devices: 116 us -> 7.6 us
    psum x1 -> x0, waiting for transfers between devices: 116 us -> none  [body(): lax.psum(jnp.dot(basis, basis.T, precision=highest), ('grp', 'row'))]
  transfers between devices with their start and end apart: 4 -> 4, of which waited for: 2 -> 1; matrix products, arithmetic and copies ran while one was open for 15% -> 2% of each run, Pallas kernels for 0% -> 0%
where the time goes in v1:
time: 1120 us
  matrix products  361 us (32%)
  local copies, waits for them, and re-layouts  352 us (31%)
  other arithmetic  176 us (16%)
  loops' own time  110 us (10%)
  blocking collectives  87.6 us (8%)
  between operations  14.4 us (1%)
    gather x16, local copies, waits for them, and re-layouts, apply_local(): picked = jnp.take(extended, positions + offsets[slot_index], axis=1)  271 us
    dot_general x144, matrix products, cholesky_step(): jnp.dot(factor, factor_row, precision=lax.Precision.HIGHEST)  117 us
    dot_general x144, matrix products, forward_step(): jnp.dot(lower_row, solved, precision=lax.Precision.HIGHEST)  115 us
    another operation x2, loops' own time, cholesky_lower(): lax.fori_loop(0, order, cholesky_step, jnp.zeros(matrix.shape, matrix.dty...  104 us
    dot_general x128, matrix products, backward_step(): jnp.dot(upper_row, solved, precision=lax.Precision.HIGHEST)  102 us
    reduce_sum x144, other arithmetic, forward_step(): jnp.sum(jnp.where(jnp.arange(order, dtype=jnp.int32) == row_index, lower_...  87.3 us
    reduce_sum x128, other arithmetic, backward_step(): jnp.sum(jnp.where(jnp.arange(order, dtype=jnp.int32) == row_index, upper_...  77.7 us
    dynamic_update_slice x144, local copies, waits for them, and re-layouts, cholesky_step(): lax.dynamic_update_slice_in_dim(factor, fresh[:, None], column_index, 1)  47.2 us
  transfers between devices with their start and end apart: 4, of which 1 were waited for; matrix products, arithmetic and copies ran while one was open for 2% of the time, Pallas kernels for 0%

profile of v1, /device:TPU:0, one launch (start us, length us, event | category | flops | bytes accessed | tf_op | source)
XLA Modules:
  0.0 1117.1 jit_solution(5591544788895336431)
XLA Ops:
  7.2 2.2 copy.72
  9.3 5.2 all-to-all-start
  14.6 7.6 fusion.64
  23.9 1.1 fusion.60
  27.0 5.1 convolution_bitcast_fusion.7
  32.1 41.2 %all-reduce.1 = (f32[128,16]{0,1:T(8,128)S(1)}, f32[16,16]{1,0:T(8,128)S(1)}) all-reduce(f32[128,16]{0,1:T(8,128)S(1)} %convolution_bitcast_fusion.7, f32[16,16]{1,0:T(8,128)S(1)} %fusion.63), channel_id=1, replica_groups=mesh['grp'=4,'row'=8] {'grp','row'}, use_global_device_ids=true, to_apply=%region_1.2 | all-reduce | flops 2304 | bytes 18432 | tf_op jit(solution)/shard_map/psum | solution.py:103
  73.4 7.6 all-gather.3.cloned.1.call-done
  81.0 1.7 reduce_sum.86
  82.8 258.7 %while.74 = (s32[]{:T(128)}, f32[128,128]{1,0:T(8,128)S(1)}, f32[128,128]{0,1:T(8,128)S(1)}, s32[]{:T(128)}, s32[]{:T(128)}) while((s32[]{:T(128)}, f32[128,128]{1,0:T(8,128)S(1)}, f32[128,128]{0,1:T(8,128)S(1)}, s32[]{:T(128)}, s32[]{:T(128)}) %tuple.198), condition=%wide.region_5.6_spmd.clone.clone, body=%wide.region_3.5_spmd.clone.clone.sunk | while | flops 197761 | bytes 71765 | solution.py:43
  82.8 0.8 fusion.125
  84.7 0.8 fusion.125
  86.8 0.8 fusion.125
  88.8 0.8 fusion.125
  90.8 0.8 fusion.125
  92.8 0.8 fusion.125
  94.8 0.8 fusion.125
  96.9 0.8 fusion.125
  98.9 0.8 fusion.125
  100.9 0.8 fusion.125
  102.9 0.8 fusion.125
  105.0 0.8 fusion.125
  107.0 0.8 fusion.125
  109.0 0.8 fusion.125
  111.0 0.8 fusion.125
  113.0 0.8 fusion.125
  115.1 0.8 fusion.125
  117.1 0.8 fusion.125
  119.1 0.8 fusion.125
  121.1 0.8 fusion.125
  123.2 0.8 fusion.125
  125.2 0.8 fusion.125
  127.2 0.8 fusion.125
  129.2 0.8 fusion.125
  131.2 0.8 fusion.125
  133.3 0.8 fusion.125
  341.6 186.3 %while.71 = (s32[]{:T(128)}, f32[128,16]{1,0:T(8,128)S(1)}, f32[128,16]{1,0:T(8,128)S(1)}, f32[128,128]{1,0:T(8,128)S(1)}, s32[]{:T(128)}, /*index=5*/s32[]{:T(128)}) while((s32[]{:T(128)}, f32[128,16]{1,0:T(8,128)S(1)}, f32[128,16]{1,0:T(8,128)S(1)}, f32[128,128]{1,0:T(8,128)S(1)}, s32[]{:T(128)}, /*index=5*/s32[]{:T(128)}) %tuple.201), condition=%wide.region_8.9_spmd, body=%wide.region_6.8_spmd.sunk | while | flops 24993 | bytes 69901 | solution.py:56
  528.0 187.1 %while.72 = (s32[]{:T(128)}, f32[128,16]{1,0:T(8,128)S(1)}, f32[128,16]{1,0:T(8,128)S(1)}, f32[128,128]{0,1:T(8,128)S(1)}, s32[]{:T(128)}, /*index=5*/s32[]{:T(128)}, s32[]{:T(128)}, s32[]{:T(128)}) while((s32[]{:T(128)}, f32[128,16]{1,0:T(8,128)S(1)}, f32[128,16]{1,0:T(8,128)S(1)}, f32[128,128]{0,1:T(8,128)S(1)}, s32[]{:T(128)}, ...), condition=%wide.region_11.12_spmd, body=%wide.region_9.11_spmd.sunk | while | flops 24997 | bytes 68439 | solution.py:70
  715.5 3.9 convolution_subtract_fusion
  719.8 26.0 %while.75 = (s32[]{:T(128)}, f32[16,16]{1,0:T(8,128)S(1)}, f32[16,16]{0,1:T(8,128)S(1)}, s32[]{:T(128)}, s32[]{:T(128)}) while((s32[]{:T(128)}, f32[16,16]{1,0:T(8,128)S(1)}, f32[16,16]{0,1:T(8,128)S(1)}, s32[]{:T(128)}, s32[]{:T(128)}) %tuple.207), condition=%wide.region_14.15_spmd.clone.clone, body=%wide.region_12.14_spmd.clone.clone.sunk | while | flops 3217 | bytes 11285 | solution.py:43
  745.8 22.8 %while.73 = (s32[]{:T(128)}, f32[16,16]{1,0:T(8,128)S(1)}, f32[16,16]{1,0:T(8,128)S(1)}, f32[16,16]{1,0:T(8,128)S(1)}, s32[]{:T(128)}, /*index=5*/s32[]{:T(128)}) while((s32[]{:T(128)}, f32[16,16]{1,0:T(8,128)S(1)}, f32[16,16]{1,0:T(8,128)S(1)}, f32[16,16]{1,0:T(8,128)S(1)}, s32[]{:T(128)}, /*index=5*/s32[]{:T(128)}) %tuple.210), condition=%wide.region_17.18_spmd, body=%wide.region_15.17_spmd.sunk | while | flops 3153 | bytes 12109 | solution.py:56
  769.2 2.2 collective-permute-start
  771.4 1.5 collective-permute-start.1
  774.8 3.9 copy.79
  778.8 30.6 %gather_fusion = f32[8192,16]{1,0:T(8,128)} fusion(f32[16,12288]{0,1:T(8,128)} %copy.79, s32[8192]{0:T(1024)S(1)} %fusion.44), kind=kCustom, calls=%fused_computation.clone | custom fusion | bytes 1081344 | tf_op jit(solution)/shard_map/jit(_take)/gather | solution.py:81
  809.4 2.8 copy.80
  812.2 30.7 %gather_fusion.1 = f32[8192,16]{1,0:T(8,128)} fusion(f32[16,12288]{0,1:T(8,128)} %copy.79, s32[8192]{0:T(1024)S(1)} %fusion.45), kind=kCustom, calls=%fused_computation.1.clone | custom fusion | bytes 1081344 | tf_op jit(solution)/shard_map/jit(_take)/gather | solution.py:81
  842.8 2.8 copy.82
  845.6 30.7 %gather_fusion.2 = f32[8192,16]{1,0:T(8,128)} fusion(f32[16,12288]{0,1:T(8,128)} %copy.79, s32[8192]{0:T(1024)S(1)} %fusion.46), kind=kCustom, calls=%fused_computation.2.clone | custom fusion | bytes 1081344 | tf_op jit(solution)/shard_map/jit(_take)/gather | solution.py:81
  876.3 2.8 copy.84
  879.1 30.7 %gather_fusion.3 = f32[8192,16]{1,0:T(8,128)} fusion(f32[16,12288]{0,1:T(8,128)} %copy.79, s32[8192]{0:T(1024)S(1)} %fusion.47), kind=kCustom, calls=%fused_computation.3.clone | custom fusion | bytes 1081344 | tf_op jit(solution)/shard_map/jit(_take)/gather | solution.py:81
  909.7 3.5 copy.86
  913.2 30.6 %gather_fusion.4 = f32[8192,16]{1,0:T(8,128)} fusion(f32[16,12288]{0,1:T(8,128)} %copy.79, s32[8192]{0:T(1024)S(1)} %fusion.48), kind=kCustom, calls=%fused_computation.4.clone | custom fusion | bytes 1081344 | tf_op jit(solution)/shard_map/jit(_take)/gather | solution.py:81
  943.9 3.5 copy.88
  947.4 30.6 %gather_fusion.5 = f32[8192,16]{1,0:T(8,128)} fusion(f32[16,12288]{0,1:T(8,128)} %copy.79, s32[8192]{0:T(1024)S(1)} %fusion.49), kind=kCustom, calls=%fused_computation.5.clone | custom fusion | bytes 1081344 | tf_op jit(solution)/shard_map/jit(_take)/gather | solution.py:81
  978.0 3.5 copy.90
  981.5 30.6 %gather_fusion.6 = f32[8192,16]{1,0:T(8,128)} fusion(f32[16,12288]{0,1:T(8,128)} %copy.79, s32[8192]{0:T(1024)S(1)} %fusion.50), kind=kCustom, calls=%fused_computation.6.clone | custom fusion | bytes 1081344 | tf_op jit(solution)/shard_map/jit(_take)/gather | solution.py:81
  1012.1 3.5 copy.92
  1015.6 30.6 %gather_fusion.7 = f32[8192,16]{1,0:T(8,128)} fusion(f32[16,12288]{0,1:T(8,128)} %copy.79, s32[8192]{0:T(1024)S(1)} %fusion.51), kind=kCustom, calls=%fused_computation.7.clone | custom fusion | bytes 1081344 | tf_op jit(solution)/shard_map/jit(_take)/gather | solution.py:81
  1046.3 3.5 copy.94
  1049.8 3.5 multiply_reduce_fusion
  1054.1 3.3 convolution_bitcast_fusion.6
  1058.2 3.4 convolution_bitcast_fusion.5
  1061.7 46.4 %all-reduce = (f32[2,144,16]{1,2,0:T(8,128)S(1)}, f32[16]{0:T(128)S(1)}) all-reduce(f32[2,144,16]{1,2,0:T(8,128)S(1)} %pad_maximum_fusion.2, f32[16]{0:T(128)S(1)} %copy-done.6), channel_id=1, replica_groups=mesh['grp'=4,'row'=8] {'grp','row'}, use_global_device_ids=true, to_apply=%region_18.20 | all-reduce | flops 4624 | bytes 36992 | tf_op jit(solution)/shard_map/psum | solution.py:132
  1109.2 1.0 pad_maximum_fusion
  (1436 shorter events, 559.5 us)
Async XLA Ops:
  9.3 16.3 %all-to-all-start = ((f32[4,4,8192]{2,0,1:T(4,128)}), f32[4,4,8192]{2,0,1:T(4,128)S(1)}, u32[]{:S(2)}, u32[]{:S(2)}) async-start(f32[4,4,8192]{2,0,1:T(4,128)} %copy.72), calls=%async_computation | async-start | bytes 1048576 | tf_op jit(solution)/shard_map/all_to_all | solution.py:95
  14.5 7.7 copy-start.3
  14.5 9.4 copy-start.2
  14.5 11.3 %copy-start.7 = (s32[16]{0:T(128)S(1)}, s32[16]{0:T(128)}, u32[]{:S(2)}) copy-start(s32[16]{0:T(128)} %param.20) | copy-start | bytes 196
  14.5 66.5 %all-gather.3.cloned.1.call-start = ((), (), s32[]{:S(2)}) async-start(), calls=%async_computation.1 | async-start | bytes 2162688 | tf_op jit(solution)/shard_map/all_gather | solution.py:10
  527.9 244.9 %copy-start.8 = (s32[16]{0:T(128)S(1)}, s32[16]{0:T(128)}, u32[]{:S(2)}) copy-start(s32[16]{0:T(128)} %param.21) | copy-start | bytes 196
  769.2 288.2 %copy-start.1 = (f32[16,8192]{1,0:T(8,128)}, f32[16,8192]{1,0:T(8,128)S(1)}, u32[]{:S(2)}) copy-start(f32[16,8192]{1,0:T(8,128)S(1)} %fusion.65) | copy-start | bytes 1572868
  769.2 5.5 collective-permute-start
  771.4 3.3 collective-permute-start.1
  1015.6 34.2 %copy-start.4 = (f32[1,1,8192]{2,1,0:T(1,128)S(1)}, f32[1,1,8192]{2,1,0:T(1,128)}, u32[]{:S(2)}) copy-start(f32[1,1,8192]{2,1,0:T(1,128)} %get-tuple-element.615) | copy-start | bytes 98308
  1015.6 34.2 %copy-start.5 = (f32[1,1,8192]{2,1,0:T(1,128)S(1)}, f32[1,1,8192]{2,1,0:T(1,128)}, u32[]{:S(2)}) copy-start(f32[1,1,8192]{2,1,0:T(1,128)} %get-tuple-element.616) | copy-start | bytes 98308
  1049.8 4.3 copy-start
  1054.1 7.6 copy-start.6
Sparse Core Ops, SparseCore 0:
  22.3 58.5 all-gather.2
